TPU v7x, 128 devices: a whole 4x4x4 slice. The times are simulated.
128 devices in a mesh: pipe: 8 (over z_lo, x), dp: 16 (over y, z_hi, core).
Axes of the slice: x: 4, y: 4, z: 4 (z_hi: 2, z_lo: 2; z = z_hi * 2 + z_lo), core: 2. Of those that a mesh axis runs over, the one named last changes fastest.
Arguments:
- section_inputs: bfloat16 [8, 3, 2048, 3072], P('pipe', None, 'dp'), may hold values from -6 to 6
- weights: bfloat16 [8, 3072, 3072], P('pipe'), may hold values from -0.109375 to 0.109375
- norm_gains: float32 [8, 3072], P('pipe'), may hold values from 0.1 to 1.9
- upstream: bfloat16 [3, 2048, 3072], P(None, 'dp'), may hold values from -4 to 4
- edge_list: int32 [3, 16, 384, 2], P(None, 'dp'), may hold values from 0 to 127
- time_steps: int32 [3, 16], P(None, 'dp'), may hold values from 0 to 999
Outputs:
- section_grads: bfloat16 [8, 3, 2048, 3072], P('pipe', None, 'dp')
- weight_grads: bfloat16 [8, 3072, 3072], P('pipe', 'dp')
Inputs may be any that keep to these rules, and one draw needn't show every extreme that they name: `edge_list`: every entry is a node number of the micro-batch's graph on that replica, from 0 to 127.
All inputs are finite; a program needn't handle non-finite values.
Results may differ from a plain program's by a relative error of at most 0.022.
Values may be sent and summed in bfloat16 or wider, within the bound.
No kernel may reach another device: no remote copies, remote signals or barrier semaphores. Data moves between devices by JAX's collectives and lax.ppermute only.
A program may use at most 192 MiB of HBM per device.

v0:
```python
import math

import jax
import jax.numpy as jnp
from jax import lax
from jax.sharding import PartitionSpec as P


def shifted(x, axis, by):
    length = lax.axis_size(axis)
    pairs = [(i, i + by) for i in range(length) if 0 <= i + by < length]
    return lax.ppermute(x, axis, pairs)


def diffusion(edge_list, node_count):
    node_ids = jnp.arange(node_count, dtype=jnp.int32)
    source = (edge_list[:, 0:1] == node_ids[None, :]).astype(jnp.float32)
    target = (edge_list[:, 1:2] == node_ids[None, :]).astype(jnp.float32)
    adjacency = lax.dot_general(
        source, target, (((0,), (0,)), ((), ())), precision=lax.Precision.HIGHEST
    )
    adjacency = adjacency + adjacency.T + jnp.eye(node_count, dtype=jnp.float32)
    degree = jnp.sum(adjacency, axis=-1, keepdims=True)
    return (adjacency / degree).astype(jnp.bfloat16)


def timestep_gate(time_steps, width):
    frequency = jnp.exp(-math.log(10000.0) * jnp.arange(width).astype(jnp.float32) / width)
    return 1.0 + 0.5 * jnp.sin(time_steps.astype(jnp.float32)[..., None] * frequency)


def recompute(hidden, mixing, norm_gain, weight):
    wide = hidden.astype(jnp.float32)
    inv_rms = lax.rsqrt(jnp.mean(wide * wide, axis=-1, keepdims=True) + 1e-06)
    normed = (wide * inv_rms * norm_gain).astype(jnp.bfloat16)
    mixed = jnp.dot(mixing, normed, preferred_element_type=jnp.float32).astype(jnp.bfloat16)
    pre_act = jnp.dot(mixed, weight, preferred_element_type=jnp.float32)
    return (mixed, pre_act, inv_rms)


def backprop(hidden, grad_out, mixing, norm_gain, weight, gate_row, pre_act, inv_rms):
    logistic = jax.nn.sigmoid(pre_act)
    slope = logistic * (1.0 + pre_act * (1.0 - logistic))
    grad_act = (grad_out.astype(jnp.float32) * gate_row * slope).astype(jnp.bfloat16)
    grad_mix = lax.dot_general(
        grad_act, weight, (((1,), (1,)), ((), ())), preferred_element_type=jnp.float32
    ).astype(jnp.bfloat16)
    grad_norm = lax.dot_general(
        mixing, grad_mix, (((0,), (0,)), ((), ())), preferred_element_type=jnp.float32
    )
    wide = hidden.astype(jnp.float32)
    scaled = grad_norm * norm_gain
    inner = jnp.mean(scaled * wide, axis=-1, keepdims=True)
    grad_in = (
        grad_out.astype(jnp.float32) + inv_rms * scaled - wide * inv_rms * inv_rms * inv_rms * inner
    )
    return (grad_in.astype(jnp.bfloat16), grad_act)


def local(section_inputs, weights, norm_gains, upstream, edge_list, time_steps):
    section_index = lax.axis_index("pipe")
    last_section = lax.axis_size("pipe") - 1
    micro_count = section_inputs.shape[1]
    node_count = section_inputs.shape[2]
    width = section_inputs.shape[3]
    hidden_all = section_inputs[0]
    weight = weights[0]
    norm_gain = norm_gains[0]
    mixing_all = jax.vmap(lambda edges_one: diffusion(edges_one, node_count))(edge_list[:, 0])
    gates_all = timestep_gate(time_steps[:, 0], width)
    extra_init = jnp.zeros((width, width), jnp.float32)
    received_init = jnp.zeros((node_count, width), jnp.bfloat16)
    outputs_init = jnp.zeros((micro_count, node_count, width), jnp.bfloat16)

    def tick(tick_idx, carry):
        received, outputs, extra = carry
        micro = tick_idx - (last_section - section_index)
        active = jnp.logical_and(micro >= 0, micro < micro_count)
        slot = jnp.clip(micro, 0, micro_count - 1)
        grad_out = jnp.where(section_index == last_section, upstream[slot], received)

        def run(operands):
            outputs_now, extra_now = operands
            hidden = hidden_all[slot]
            mixing = mixing_all[slot]
            mixed, pre_act, inv_rms = recompute(hidden, mixing, norm_gain, weight)
            grad_in, grad_act = backprop(
                hidden, grad_out, mixing, norm_gain, weight, gates_all[slot], pre_act, inv_rms
            )
            outputs_now = lax.dynamic_update_index_in_dim(outputs_now, grad_in, slot, 0)
            extra_now = extra_now + lax.dot_general(
                mixed, grad_act, (((0,), (0,)), ((), ())), preferred_element_type=jnp.float32
            )
            return (grad_in, outputs_now, extra_now)

        def skip(operands):
            return (jnp.zeros_like(received), operands[0], operands[1])

        grad_in, outputs, extra = lax.cond(active, run, skip, (outputs, extra))
        received = shifted(grad_in, "pipe", -1)
        return (received, outputs, extra)

    received, outputs, extra = lax.fori_loop(
        0, micro_count + last_section, tick, (received_init, outputs_init, extra_init)
    )
    weight_rows = lax.psum_scatter(
        extra.astype(jnp.bfloat16), "dp", scatter_dimension=0, tiled=True
    )
    return (outputs[None], weight_rows[None])


def solution(mesh):
    in_specs = (
        P("pipe", None, "dp", None),
        P("pipe", None, None),
        P("pipe", None),
        P(None, "dp", None),
        P(None, "dp", None, None),
        P(None, "dp"),
    )
    out_specs = (P("pipe", None, "dp", None), P("pipe", "dp", None))
    return jax.shard_map(local, mesh=mesh, in_specs=in_specs, out_specs=out_specs, check_vma=False)
```

profile of v0, /device:TPU:18, one launch (start us, length us, event | category | flops | bytes accessed | tf_op | source)
XLA Modules:
  0.0 990.8 jit_solution(10656571379894721861)
XLA Ops:
  9.3 12.5 %broadcast_in_dim.28 = f32[3072,3072]{1,0:T(8,128)} broadcast(f32[]{:T(128)} %constant.107.clone.1), dimensions={} | broadcast | bytes 37748740 | tf_op jit(solution)/shard_map/broadcast_in_dim | solution.py:71
  24.5 779.9 %while.20 = (s32[]{:T(128)}, bf16[128,3072]{1,0:T(8,128)(2,1)}, bf16[3,128,3072]{2,1,0:T(8,128)(2,1)}, f32[3072,3072]{1,0:T(8,128)}, s32[]{:T(128)}, /*index=5*/...) while((s32[]{:T(128)}, bf16[128,3072]{1,0:T(8,128)(2,1)}, ...), condition=%wide.region_6.7_spmd.clone, body=%wide.region_1.6_spmd.clone.sunk | while | flops 7476618240 | bytes 142490576 | solution.py:103
  27.9 18.9 %collective-permute-done = bf16[128,3072]{1,0:T(8,128)(2,1)S(1)} collective-permute-done((bf16[128,3072]{1,0:T(8,128)(2,1)}, bf16[128,3072]{1,0:T(8,128)(2,1)S(1)}, u32[]{:S(2)}, u32[]{:S(2)}) %collective-permute-start) | collective-permute-done | bytes 786464 | tf_op jit(solution)/shard_map/while/body/eval_jaxpr/ppermute | solution.py:12
  51.1 18.1 %collective-permute-done = bf16[128,3072]{1,0:T(8,128)(2,1)S(1)} collective-permute-done((bf16[128,3072]{1,0:T(8,128)(2,1)}, bf16[128,3072]{1,0:T(8,128)(2,1)S(1)}, u32[]{:S(2)}, u32[]{:S(2)}) %collective-permute-start) | collective-permute-done | bytes 786464 | tf_op jit(solution)/shard_map/while/body/eval_jaxpr/ppermute | solution.py:12
  73.5 18.7 %collective-permute-done = bf16[128,3072]{1,0:T(8,128)(2,1)S(1)} collective-permute-done((bf16[128,3072]{1,0:T(8,128)(2,1)}, bf16[128,3072]{1,0:T(8,128)(2,1)S(1)}, u32[]{:S(2)}, u32[]{:S(2)}) %collective-permute-start) | collective-permute-done | bytes 786464 | tf_op jit(solution)/shard_map/while/body/eval_jaxpr/ppermute | solution.py:12
  96.0 18.8 %collective-permute-done = bf16[128,3072]{1,0:T(8,128)(2,1)S(1)} collective-permute-done((bf16[128,3072]{1,0:T(8,128)(2,1)}, bf16[128,3072]{1,0:T(8,128)(2,1)S(1)}, u32[]{:S(2)}, u32[]{:S(2)}) %collective-permute-start) | collective-permute-done | bytes 786464 | tf_op jit(solution)/shard_map/while/body/eval_jaxpr/ppermute | solution.py:12
  118.6 17.9 %collective-permute-done = bf16[128,3072]{1,0:T(8,128)(2,1)S(1)} collective-permute-done((bf16[128,3072]{1,0:T(8,128)(2,1)}, bf16[128,3072]{1,0:T(8,128)(2,1)S(1)}, u32[]{:S(2)}, u32[]{:S(2)}) %collective-permute-start) | collective-permute-done | bytes 786464 | tf_op jit(solution)/shard_map/while/body/eval_jaxpr/ppermute | solution.py:12
  140.2 358.4 %collective-permute-done = bf16[128,3072]{1,0:T(8,128)(2,1)S(1)} collective-permute-done((bf16[128,3072]{1,0:T(8,128)(2,1)}, bf16[128,3072]{1,0:T(8,128)(2,1)S(1)}, u32[]{:S(2)}, u32[]{:S(2)}) %collective-permute-start) | collective-permute-done | bytes 786464 | tf_op jit(solution)/shard_map/while/body/eval_jaxpr/ppermute | solution.py:12
  499.5 58.8 %conditional.3 = (bf16[128,3072]{1,0:T(8,128)(2,1)}, bf16[3,128,3072]{2,1,0:T(8,128)(2,1)}, f32[3072,3072]{1,0:T(8,128)}) conditional(s32[]{:T(128)} %convert_element_type.174, (bf16[3,128,3072]{2,1,0:T(8,128)(2,1)}, f32[3072,3072]{1,0:T(8,128)}) %tuple.77, (pred[]{:T(512)}, s32[]{:T(128)}, bf16[3,128,3072]{2,1,0:T(8,128)(2,1)}, ...), branch_computations={%region_2.2_spmd, %region_3.5_spmd.clone} | conditional | flops 7476618240 | bytes 136198752 | solution.py:99
  513.2 27.5 %convolution_add_fusion = f32[3072,3072]{1,0:T(8,128)} fusion(f32[3072,3072]{1,0:T(8,128)} %get-tuple-element.448, bf16[128,3072]{1,0:T(8,128)(2,1)S(1)} %convolution_convert_fusion.1, bf16[128,3072]{1,0:T(8,128)(2,1)S(1)} %bitcast_select_fusion, f32[128,3072]{1,0:T(8,128)S(1)} %fusion.56, f32[3072]{0:T(1024)S(1)} %bitcast.67), kind=kOutput, calls=%fused_computation.1 | convolution fusion | flops 2429681664 | bytes 78655488 | tf_op jit(solution)/shard_map/while/body/eval_jaxpr/cond/branch_1_fun/dot_general | solution.py:91
  540.7 14.2 %fusion.13 = (f32[128]{0:T(128)S(1)}, f32[128,3072]{1,0:T(8,128)}) fusion(bf16[3,128,3072]{2,1,0:T(8,128)(2,1)} %get-tuple-element.443, s32[]{:T(128)S(6)} %min.12, f32[3072]{0:T(1024)S(1)} %bitcast.70, bf16[3072,3072]{1,0:T(8,128)(2,1)} %get-tuple-element.446, bf16[128,3072]{1,0:T(8,128)(2,1)S(1)} %bitcast_select_fusion, f32[128,3072]{1,0:T(8,128)S(1)} %fusion.56, ...), kind=kOutput, calls=%fused_computation.20 | convolution fusion | flops 2522873856 | bytes 23651840 | tf_op jit(solution)/shard_map/while/body/eval_jaxpr/cond/branch_1_fun/dot_general | solution.py:48
  560.2 17.2 %collective-permute-done = bf16[128,3072]{1,0:T(8,128)(2,1)S(1)} collective-permute-done((bf16[128,3072]{1,0:T(8,128)(2,1)}, bf16[128,3072]{1,0:T(8,128)(2,1)S(1)}, u32[]{:S(2)}, u32[]{:S(2)}) %collective-permute-start) | collective-permute-done | bytes 786464 | tf_op jit(solution)/shard_map/while/body/eval_jaxpr/ppermute | solution.py:12
  578.3 58.8 %conditional.3 = (bf16[128,3072]{1,0:T(8,128)(2,1)}, bf16[3,128,3072]{2,1,0:T(8,128)(2,1)}, f32[3072,3072]{1,0:T(8,128)}) conditional(s32[]{:T(128)} %convert_element_type.174, (bf16[3,128,3072]{2,1,0:T(8,128)(2,1)}, f32[3072,3072]{1,0:T(8,128)}) %tuple.77, (pred[]{:T(512)}, s32[]{:T(128)}, bf16[3,128,3072]{2,1,0:T(8,128)(2,1)}, ...), branch_computations={%region_2.2_spmd, %region_3.5_spmd.clone} | conditional | flops 7476618240 | bytes 136198752 | solution.py:99
  592.0 27.5 %convolution_add_fusion = f32[3072,3072]{1,0:T(8,128)} fusion(f32[3072,3072]{1,0:T(8,128)} %get-tuple-element.448, bf16[128,3072]{1,0:T(8,128)(2,1)S(1)} %convolution_convert_fusion.1, bf16[128,3072]{1,0:T(8,128)(2,1)S(1)} %bitcast_select_fusion, f32[128,3072]{1,0:T(8,128)S(1)} %fusion.56, f32[3072]{0:T(1024)S(1)} %bitcast.67), kind=kOutput, calls=%fused_computation.1 | convolution fusion | flops 2429681664 | bytes 78655488 | tf_op jit(solution)/shard_map/while/body/eval_jaxpr/cond/branch_1_fun/dot_general | solution.py:91
  619.5 14.2 %fusion.13 = (f32[128]{0:T(128)S(1)}, f32[128,3072]{1,0:T(8,128)}) fusion(bf16[3,128,3072]{2,1,0:T(8,128)(2,1)} %get-tuple-element.443, s32[]{:T(128)S(6)} %min.12, f32[3072]{0:T(1024)S(1)} %bitcast.70, bf16[3072,3072]{1,0:T(8,128)(2,1)} %get-tuple-element.446, bf16[128,3072]{1,0:T(8,128)(2,1)S(1)} %bitcast_select_fusion, f32[128,3072]{1,0:T(8,128)S(1)} %fusion.56, ...), kind=kOutput, calls=%fused_computation.20 | convolution fusion | flops 2522873856 | bytes 23651840 | tf_op jit(solution)/shard_map/while/body/eval_jaxpr/cond/branch_1_fun/dot_general | solution.py:48
  639.0 16.3 %collective-permute-done = bf16[128,3072]{1,0:T(8,128)(2,1)S(1)} collective-permute-done((bf16[128,3072]{1,0:T(8,128)(2,1)}, bf16[128,3072]{1,0:T(8,128)(2,1)S(1)}, u32[]{:S(2)}, u32[]{:S(2)}) %collective-permute-start) | collective-permute-done | bytes 786464 | tf_op jit(solution)/shard_map/while/body/eval_jaxpr/ppermute | solution.py:12
  656.2 58.8 %conditional.3 = (bf16[128,3072]{1,0:T(8,128)(2,1)}, bf16[3,128,3072]{2,1,0:T(8,128)(2,1)}, f32[3072,3072]{1,0:T(8,128)}) conditional(s32[]{:T(128)} %convert_element_type.174, (bf16[3,128,3072]{2,1,0:T(8,128)(2,1)}, f32[3072,3072]{1,0:T(8,128)}) %tuple.77, (pred[]{:T(512)}, s32[]{:T(128)}, bf16[3,128,3072]{2,1,0:T(8,128)(2,1)}, ...), branch_computations={%region_2.2_spmd, %region_3.5_spmd.clone} | conditional | flops 7476618240 | bytes 136198752 | solution.py:99
  669.9 27.5 %convolution_add_fusion = f32[3072,3072]{1,0:T(8,128)} fusion(f32[3072,3072]{1,0:T(8,128)} %get-tuple-element.448, bf16[128,3072]{1,0:T(8,128)(2,1)S(1)} %convolution_convert_fusion.1, bf16[128,3072]{1,0:T(8,128)(2,1)S(1)} %bitcast_select_fusion, f32[128,3072]{1,0:T(8,128)S(1)} %fusion.56, f32[3072]{0:T(1024)S(1)} %bitcast.67), kind=kOutput, calls=%fused_computation.1 | convolution fusion | flops 2429681664 | bytes 78655488 | tf_op jit(solution)/shard_map/while/body/eval_jaxpr/cond/branch_1_fun/dot_general | solution.py:91
  697.5 14.2 %fusion.13 = (f32[128]{0:T(128)S(1)}, f32[128,3072]{1,0:T(8,128)}) fusion(bf16[3,128,3072]{2,1,0:T(8,128)(2,1)} %get-tuple-element.443, s32[]{:T(128)S(6)} %min.12, f32[3072]{0:T(1024)S(1)} %bitcast.70, bf16[3072,3072]{1,0:T(8,128)(2,1)} %get-tuple-element.446, bf16[128,3072]{1,0:T(8,128)(2,1)S(1)} %bitcast_select_fusion, f32[128,3072]{1,0:T(8,128)S(1)} %fusion.56, ...), kind=kOutput, calls=%fused_computation.20 | convolution fusion | flops 2522873856 | bytes 23651840 | tf_op jit(solution)/shard_map/while/body/eval_jaxpr/cond/branch_1_fun/dot_general | solution.py:48
  717.0 14.0 %collective-permute-done = bf16[128,3072]{1,0:T(8,128)(2,1)S(1)} collective-permute-done((bf16[128,3072]{1,0:T(8,128)(2,1)}, bf16[128,3072]{1,0:T(8,128)(2,1)S(1)}, u32[]{:S(2)}, u32[]{:S(2)}) %collective-permute-start) | collective-permute-done | bytes 786464 | tf_op jit(solution)/shard_map/while/body/eval_jaxpr/ppermute | solution.py:12
  732.7 59.9 %collective-permute-start = (bf16[128,3072]{1,0:T(8,128)(2,1)}, bf16[128,3072]{1,0:T(8,128)(2,1)S(1)}, u32[]{:S(2)}, u32[]{:S(2)}) collective-permute-start(bf16[128,3072]{1,0:T(8,128)(2,1)} %get-tuple-element.579), channel_id=1, source_target_pairs={{16,0},{32,16},{48,32},{64,48},{80,64},{96,80},{112,96},{17,1},{33... | collective-permute-start | bytes 2359304 | tf_op jit(solution)/shard_map/while/body/eval_jaxpr/ppermute | solution.py:12
  792.7 10.8 %collective-permute-done = bf16[128,3072]{1,0:T(8,128)(2,1)S(1)} collective-permute-done((bf16[128,3072]{1,0:T(8,128)(2,1)}, bf16[128,3072]{1,0:T(8,128)(2,1)S(1)}, u32[]{:S(2)}, u32[]{:S(2)}) %collective-permute-start) | collective-permute-done | bytes 786464 | tf_op jit(solution)/shard_map/while/body/eval_jaxpr/ppermute | solution.py:12
  804.4 20.7 %convert_element_type.95 = bf16[3072,3072]{1,0:T(8,128)(2,1)} convert(f32[3072,3072]{1,0:T(8,128)} %get-tuple-element.394) | non-fusion elementwise | flops 9437184 | bytes 56623104 | tf_op jit(solution)/shard_map/convert_element_type | solution.py:107
  825.2 158.8 %reduce-scatter.2.cloned.1.call-done = bf16[192,3072]{1,0:T(8,128)(2,1)} async-done(((bf16[3072,3072]{1,0:T(8,128)(2,1)}), bf16[192,3072]{1,0:T(8,128)(2,1)}) %reduce-scatter.2.cloned.1.call-update) | async-done | bytes 1179664 | tf_op jit(solution)/shard_map/reduce_scatter | solution.py:106
  (90 shorter events, 96.8 us)
Async XLA Ops:
  7.2 976.8 %reduce-scatter.2.cloned.1.call-start = ((), (), s32[]{:S(2)}) async-start(), calls=%async_computation.1 | async-start | bytes 20054016 | tf_op jit(solution)/shard_map/reduce_scatter | solution.py:106
  21.9 2.6 copy-start.2
  25.5 21.4 %collective-permute-start = (bf16[128,3072]{1,0:T(8,128)(2,1)}, bf16[128,3072]{1,0:T(8,128)(2,1)S(1)}, u32[]{:S(2)}, u32[]{:S(2)}) collective-permute-start(bf16[128,3072]{1,0:T(8,128)(2,1)} %get-tuple-element.579), channel_id=1, source_target_pairs={{16,0},{32,16},{48,32},{64,48},{80,64},{96,80},{112,96},{17,1},{33... | collective-permute-start | bytes 2359304 | tf_op jit(solution)/shard_map/while/body/eval_jaxpr/ppermute | solution.py:12
  46.9 0.9 copy-start.1
  48.7 20.5 %collective-permute-start = (bf16[128,3072]{1,0:T(8,128)(2,1)}, bf16[128,3072]{1,0:T(8,128)(2,1)S(1)}, u32[]{:S(2)}, u32[]{:S(2)}) collective-permute-start(bf16[128,3072]{1,0:T(8,128)(2,1)} %get-tuple-element.579), channel_id=1, source_target_pairs={{16,0},{32,16},{48,32},{64,48},{80,64},{96,80},{112,96},{17,1},{33... | collective-permute-start | bytes 2359304 | tf_op jit(solution)/shard_map/while/body/eval_jaxpr/ppermute | solution.py:12
  69.2 0.9 copy-start.1
  71.0 21.2 %collective-permute-start = (bf16[128,3072]{1,0:T(8,128)(2,1)}, bf16[128,3072]{1,0:T(8,128)(2,1)S(1)}, u32[]{:S(2)}, u32[]{:S(2)}) collective-permute-start(bf16[128,3072]{1,0:T(8,128)(2,1)} %get-tuple-element.579), channel_id=1, source_target_pairs={{16,0},{32,16},{48,32},{64,48},{80,64},{96,80},{112,96},{17,1},{33... | collective-permute-start | bytes 2359304 | tf_op jit(solution)/shard_map/while/body/eval_jaxpr/ppermute | solution.py:12
  92.2 0.9 copy-start.1
  94.0 20.8 %collective-permute-start = (bf16[128,3072]{1,0:T(8,128)(2,1)}, bf16[128,3072]{1,0:T(8,128)(2,1)S(1)}, u32[]{:S(2)}, u32[]{:S(2)}) collective-permute-start(bf16[128,3072]{1,0:T(8,128)(2,1)} %get-tuple-element.579), channel_id=1, source_target_pairs={{16,0},{32,16},{48,32},{64,48},{80,64},{96,80},{112,96},{17,1},{33... | collective-permute-start | bytes 2359304 | tf_op jit(solution)/shard_map/while/body/eval_jaxpr/ppermute | solution.py:12
  114.8 0.9 copy-start.1
  116.6 19.8 %collective-permute-start = (bf16[128,3072]{1,0:T(8,128)(2,1)}, bf16[128,3072]{1,0:T(8,128)(2,1)S(1)}, u32[]{:S(2)}, u32[]{:S(2)}) collective-permute-start(bf16[128,3072]{1,0:T(8,128)(2,1)} %get-tuple-element.579), channel_id=1, source_target_pairs={{16,0},{32,16},{48,32},{64,48},{80,64},{96,80},{112,96},{17,1},{33... | collective-permute-start | bytes 2359304 | tf_op jit(solution)/shard_map/while/body/eval_jaxpr/ppermute | solution.py:12
  136.5 0.9 copy-start.1
  138.3 360.3 %collective-permute-start = (bf16[128,3072]{1,0:T(8,128)(2,1)}, bf16[128,3072]{1,0:T(8,128)(2,1)S(1)}, u32[]{:S(2)}, u32[]{:S(2)}) collective-permute-start(bf16[128,3072]{1,0:T(8,128)(2,1)} %get-tuple-element.579), channel_id=1, source_target_pairs={{16,0},{32,16},{48,32},{64,48},{80,64},{96,80},{112,96},{17,1},{33... | collective-permute-start | bytes 2359304 | tf_op jit(solution)/shard_map/while/body/eval_jaxpr/ppermute | solution.py:12
  498.6 0.9 copy-start.1
  502.5 7.9 copy-start
  558.3 19.1 %collective-permute-start = (bf16[128,3072]{1,0:T(8,128)(2,1)}, bf16[128,3072]{1,0:T(8,128)(2,1)S(1)}, u32[]{:S(2)}, u32[]{:S(2)}) collective-permute-start(bf16[128,3072]{1,0:T(8,128)(2,1)} %get-tuple-element.579), channel_id=1, source_target_pairs={{16,0},{32,16},{48,32},{64,48},{80,64},{96,80},{112,96},{17,1},{33... | collective-permute-start | bytes 2359304 | tf_op jit(solution)/shard_map/while/body/eval_jaxpr/ppermute | solution.py:12
  577.4 0.9 copy-start.1
  581.3 7.9 copy-start
  637.1 18.2 %collective-permute-start = (bf16[128,3072]{1,0:T(8,128)(2,1)}, bf16[128,3072]{1,0:T(8,128)(2,1)S(1)}, u32[]{:S(2)}, u32[]{:S(2)}) collective-permute-start(bf16[128,3072]{1,0:T(8,128)(2,1)} %get-tuple-element.579), channel_id=1, source_target_pairs={{16,0},{32,16},{48,32},{64,48},{80,64},{96,80},{112,96},{17,1},{33... | collective-permute-start | bytes 2359304 | tf_op jit(solution)/shard_map/while/body/eval_jaxpr/ppermute | solution.py:12
  655.4 0.9 copy-start.1
  659.2 7.9 copy-start
  715.0 15.9 %collective-permute-start = (bf16[128,3072]{1,0:T(8,128)(2,1)}, bf16[128,3072]{1,0:T(8,128)(2,1)S(1)}, u32[]{:S(2)}, u32[]{:S(2)}) collective-permute-start(bf16[128,3072]{1,0:T(8,128)(2,1)} %get-tuple-element.579), channel_id=1, source_target_pairs={{16,0},{32,16},{48,32},{64,48},{80,64},{96,80},{112,96},{17,1},{33... | collective-permute-start | bytes 2359304 | tf_op jit(solution)/shard_map/while/body/eval_jaxpr/ppermute | solution.py:12
  730.9 0.9 copy-start.1
  732.7 70.8 %collective-permute-start = (bf16[128,3072]{1,0:T(8,128)(2,1)}, bf16[128,3072]{1,0:T(8,128)(2,1)S(1)}, u32[]{:S(2)}, u32[]{:S(2)}) collective-permute-start(bf16[128,3072]{1,0:T(8,128)(2,1)} %get-tuple-element.579), channel_id=1, source_target_pairs={{16,0},{32,16},{48,32},{64,48},{80,64},{96,80},{112,96},{17,1},{33... | collective-permute-start | bytes 2359304 | tf_op jit(solution)/shard_map/while/body/eval_jaxpr/ppermute | solution.py:12
  (1 other events, 0.9 us)
Sparse Core Ops, SparseCore 0:
  825.3 158.6 reduce-scatter.1
where the time goes:
time: 994 us; the launch traced here: 991 us
  waiting for transfers between devices  668 us (67%)
  matrix products  154 us (15%)
  starting transfers between devices  78.7 us (8%)
  other arithmetic  42.4 us (4%)
  local copies, waits for them, and re-layouts  33.4 us (3%)
  between operations  14.1 us (1%)
    ppermute x10, waiting for transfers between devices, shifted(): return lax.ppermute(x, axis, pairs)  509 us
    reduce_scatter x1, waiting for transfers between devices, local(): lax.psum_scatter(extra.astype(jnp.bfloat16), 'dp', scatter_dimension=0, t...  159 us
    dot_general x3, matrix products, run(): lax.dot_general(mixed, grad_act, (((0,), (0,)), ((), ())), preferred_elem...  82.6 us
    ppermute x10, starting transfers between devices, shifted(): return lax.ppermute(x, axis, pairs)  78.7 us
    dot_general x3, matrix products, backprop(): lax.dot_general(mixing, grad_mix, (((0,), (0,)), ((), ())), preferred_ele...  42.6 us
    dot_general x3, matrix products, recompute(): pre_act = jnp.dot(mixed, weight, preferred_element_type=jnp.float32)  23.6 us
    convert_element_type x1, other arithmetic, local(): extra.astype(jnp.bfloat16)  20.7 us
  transfers between devices with their start and end apart: 11, of which 11 were waited for; matrix products, arithmetic and copies ran while one was open for 0% of the time, Pallas kernels for 0%

commit v1 on v0

v1 whole, which is shorter than its diff:
```python
import functools
import math

import jax
import jax.numpy as jnp
from jax import lax
from jax.experimental import pallas as pl
from jax.experimental.pallas import tpu as pltpu
from jax.sharding import PartitionSpec as P

VMEM_LIMIT = 36 * 1024 * 1024
NT = (((1,), (1,)), ((), ()))


def timestep_gate(time_steps, width):
    frequency = jnp.exp(-math.log(10000.0) * jnp.arange(width).astype(jnp.float32) / width)
    return 1.0 + 0.5 * jnp.sin(time_steps.astype(jnp.float32)[..., None] * frequency)


def recompute_kernel(hidden_ref, edge_ref, gate_ref, gain_ref, w_ref,
                     mixed_ref, slope_ref, mixt_ref, inv_ref, grads_ref, act_ref, mixed_s):
    del grads_ref, act_ref
    micros, nodes, width = hidden_ref.shape

    @pl.when(pl.program_id(0) == 0)
    def _():
        edges = edge_ref.shape[2]
        ids = lax.broadcasted_iota(jnp.int32, (nodes, edges), 0)
        rows = lax.broadcasted_iota(jnp.int32, (nodes, nodes), 0)
        cols = lax.broadcasted_iota(jnp.int32, (nodes, nodes), 1)
        eye = jnp.where(rows == cols, 1.0, 0.0)
        for k in range(micros):
            src = jnp.where(edge_ref[k, 0:1, :] == ids, 1.0, 0.0).astype(jnp.bfloat16)
            tgt = jnp.where(edge_ref[k, 1:2, :] == ids, 1.0, 0.0).astype(jnp.bfloat16)
            adj = lax.dot_general(src, tgt, NT, preferred_element_type=jnp.float32)
            adj = adj + lax.dot_general(tgt, src, NT, preferred_element_type=jnp.float32) + eye
            mix = adj / jnp.sum(adj, axis=-1, keepdims=True)
            mixt_ref[k] = mix.T.astype(jnp.bfloat16)
            wide = hidden_ref[k].astype(jnp.float32)
            inv = lax.rsqrt(jnp.mean(wide * wide, axis=-1, keepdims=True) + 1e-06)
            inv_ref[k] = jnp.broadcast_to(inv, (nodes, 128))
            normed = (wide * inv * gain_ref[...]).astype(jnp.bfloat16)
            mixed = jnp.dot(mix.astype(jnp.bfloat16), normed, preferred_element_type=jnp.float32)
            mixed = mixed.astype(jnp.bfloat16)
            mixed_s[pl.ds(k * nodes, nodes), :] = mixed
            mixed_ref[k] = mixed

    u = jnp.dot(mixed_s[...], w_ref[...], preferred_element_type=jnp.float32)
    logistic = jax.nn.sigmoid(u)
    slope = logistic * (1.0 + u * (1.0 - logistic))
    for k in range(micros):
        slope_ref[k] = slope[k * nodes:(k + 1) * nodes, :] * gate_ref[pl.ds(k, 1), :]


def recompute(hidden, edges_t, gates, gain, weight):
    micros, nodes, width = hidden.shape
    block = 512
    whole3 = lambda j: (0, 0, 0)
    return pl.pallas_call(
        recompute_kernel,
        grid=(width // block,),
        in_specs=[
            pl.BlockSpec((micros, nodes, width), whole3),
            pl.BlockSpec(edges_t.shape, whole3),
            pl.BlockSpec((micros, block), lambda j: (0, j)),
            pl.BlockSpec((1, width), lambda j: (0, 0)),
            pl.BlockSpec((width, block), lambda j: (0, j)),
        ],
        out_specs=[
            pl.BlockSpec((micros, nodes, width), whole3),
            pl.BlockSpec((micros, nodes, block), lambda j: (0, 0, j)),
            pl.BlockSpec((micros, nodes, nodes), whole3),
            pl.BlockSpec((micros, nodes, 128), whole3),
            pl.BlockSpec(memory_space=pl.ANY),
            pl.BlockSpec(memory_space=pl.ANY),
        ],
        out_shape=[
            jax.ShapeDtypeStruct((micros, nodes, width), jnp.bfloat16),
            jax.ShapeDtypeStruct((micros, nodes, width), jnp.float32),
            jax.ShapeDtypeStruct((micros, nodes, nodes), jnp.bfloat16),
            jax.ShapeDtypeStruct((micros, nodes, 128), jnp.float32),
            jax.ShapeDtypeStruct((micros, nodes, width), jnp.bfloat16),
            jax.ShapeDtypeStruct((micros, nodes, width), jnp.bfloat16),
        ],
        scratch_shapes=[pltpu.VMEM((micros * nodes, width), jnp.bfloat16)],
        compiler_params=pltpu.CompilerParams(vmem_limit_bytes=VMEM_LIMIT),
        cost_estimate=pl.CostEstimate(
            flops=2 * micros * nodes * width * width,
            bytes_accessed=2 * width * width + 10 * micros * nodes * width,
            transcendentals=micros * nodes * width),
        name="recompute",
    )(hidden, edges_t, gates, gain, weight)


def tick_kernel(sc_ref, recv_ref, up_ref, slope_ref, mixt_ref, hidden_ref, inv_ref, gain_ref,
                w_ref, grads_in, act_in, out_ref, grads_ref, act_ref,
                g_s, act_s, a_s, z_s, inner_s, sems):
    del grads_in, act_in
    j = pl.program_id(0)
    steps = pl.num_programs(0)
    block = w_ref.shape[0]
    width = w_ref.shape[1]
    active = sc_ref[0] == 1
    slot = sc_ref[1]
    last = sc_ref[2] == 1

    @pl.when(jnp.logical_and(active, j == 0))
    def _():
        @pl.when(last)
        def _():
            pltpu.make_async_copy(up_ref.at[slot], g_s, sems.at[0]).start()

        @pl.when(jnp.logical_not(last))
        def _():
            pltpu.make_async_copy(recv_ref.at[0], g_s, sems.at[0]).start()

        pltpu.make_async_copy(recv_ref.at[0], g_s, sems.at[0]).wait()
        act = (g_s[...].astype(jnp.float32) * slope_ref[0]).astype(jnp.bfloat16)
        act_s[...] = act
        pltpu.make_async_copy(act_s, act_ref.at[slot], sems.at[1]).start()
        a_s[...] = jnp.dot(mixt_ref[0], act, preferred_element_type=jnp.float32).astype(jnp.bfloat16)
        inner_s[...] = jnp.zeros_like(inner_s)

    @pl.when(active)
    def _():
        at = pl.ds(pl.multiple_of(j * block, block), block)
        z = lax.dot_general(a_s[...], w_ref[...], NT, preferred_element_type=jnp.float32)
        z = z * gain_ref[:, at]
        z_s[:, at] = z
        part = jnp.sum(z * hidden_ref[0, :, at].astype(jnp.float32), axis=-1, keepdims=True)
        inner_s[...] += jnp.broadcast_to(part, inner_s.shape)

    @pl.when(jnp.logical_and(active, j == steps - 1))
    def _():
        inv = inv_ref[0, :, 0:1]
        scale = inv * inv * inv * (inner_s[:, 0:1] * (1.0 / width))
        grad = (g_s[...].astype(jnp.float32) + inv * z_s[...]
                - hidden_ref[0].astype(jnp.float32) * scale)
        out_ref[0] = grad.astype(jnp.bfloat16)
        copy = pltpu.make_async_copy(out_ref.at[0], grads_ref.at[slot], sems.at[2])
        copy.start()
        pltpu.make_async_copy(act_s, act_ref.at[slot], sems.at[1]).wait()
        copy.wait()


def tick(scalars, received, upstream, slope, mixt, hidden, inv, gain, weight, grads, act):
    micros, nodes, width = hidden.shape
    block = 512
    at_slot = lambda j, sc: (sc[1], 0, 0)
    return pl.pallas_call(
        tick_kernel,
        grid_spec=pltpu.PrefetchScalarGridSpec(
            num_scalar_prefetch=1,
            grid=(width // block,),
            in_specs=[
                pl.BlockSpec(memory_space=pl.ANY),
                pl.BlockSpec(memory_space=pl.ANY),
                pl.BlockSpec((1, nodes, width), at_slot),
                pl.BlockSpec((1, nodes, nodes), at_slot),
                pl.BlockSpec((1, nodes, width), at_slot),
                pl.BlockSpec((1, nodes, 128), at_slot),
                pl.BlockSpec((1, width), lambda j, sc: (0, 0)),
                pl.BlockSpec((block, width), lambda j, sc: (j * sc[0], 0)),
                pl.BlockSpec(memory_space=pl.ANY),
                pl.BlockSpec(memory_space=pl.ANY),
            ],
            out_specs=[
                pl.BlockSpec((1, nodes, width), lambda j, sc: (0, 0, 0)),
                pl.BlockSpec(memory_space=pl.ANY),
                pl.BlockSpec(memory_space=pl.ANY),
            ],
            scratch_shapes=[
                pltpu.VMEM((nodes, width), jnp.bfloat16),
                pltpu.VMEM((nodes, width), jnp.bfloat16),
                pltpu.VMEM((nodes, width), jnp.bfloat16),
                pltpu.VMEM((nodes, width), jnp.float32),
                pltpu.VMEM((nodes, 128), jnp.float32),
                pltpu.SemaphoreType.DMA((3,)),
            ],
        ),
        out_shape=[
            jax.ShapeDtypeStruct((1, nodes, width), jnp.bfloat16),
            jax.ShapeDtypeStruct(grads.shape, grads.dtype),
            jax.ShapeDtypeStruct(act.shape, act.dtype),
        ],
        input_output_aliases={9: 1, 10: 2},
        compiler_params=pltpu.CompilerParams(vmem_limit_bytes=VMEM_LIMIT),
        cost_estimate=pl.CostEstimate(
            flops=2 * nodes * width * width,
            bytes_accessed=2 * width * width + 12 * nodes * width,
            transcendentals=0),
        name="tick",
    )(scalars, received, upstream, slope, mixt, hidden, inv, gain, weight, grads, act)


def local(section_inputs, weights, norm_gains, upstream, edge_list, time_steps):
    section = lax.axis_index("pipe")
    sections = lax.axis_size("pipe")
    micros = section_inputs.shape[1]
    width = section_inputs.shape[3]
    hidden = section_inputs[0]
    weight = weights[0]
    gates = timestep_gate(time_steps[:, 0], width)
    edges_t = jnp.swapaxes(edge_list[:, 0], 1, 2)
    mixed, slope, mixt, inv, grads, act = recompute(hidden, edges_t, gates, norm_gains, weight)

    received = upstream
    is_last = (section == sections - 1).astype(jnp.int32)
    ticks = sections + micros - 1
    for t in range(ticks):
        micro = t - (sections - 1 - section)
        active = jnp.logical_and(micro >= 0, micro < micros).astype(jnp.int32)
        scalars = jnp.stack([active, jnp.clip(micro, 0, micros - 1), is_last])
        sent, grads, act = tick(scalars, received, upstream, slope, mixt, hidden, inv,
                                norm_gains, weight, grads, act)
        if t < ticks - 1:
            pairs = [(s, s - 1) for s in range(1, sections)
                     if 0 <= t - (sections - 1 - s) < micros]
            received = lax.ppermute(sent, "pipe", pairs)

    partial = lax.dot_general(mixed.reshape(-1, width), act.reshape(-1, width),
                              (((0,), (0,)), ((), ())), preferred_element_type=jnp.float32)
    rows = lax.psum_scatter(partial.astype(jnp.bfloat16), "dp", scatter_dimension=0, tiled=True)
    return (grads[None], rows[None])


def solution(mesh):
    in_specs = (
        P("pipe", None, "dp", None),
        P("pipe", None, None),
        P("pipe", None),
        P(None, "dp", None),
        P(None, "dp", None, None),
        P(None, "dp"),
    )
    out_specs = (P("pipe", None, "dp", None), P("pipe", "dp", None))
    return jax.shard_map(local, mesh=mesh, in_specs=in_specs, out_specs=out_specs, check_vma=False)
```

time: 994 us -> 589 us (0.59)
  waiting for transfers between devices: 668 us -> 391 us
  matrix products: 154 us -> 14.7 us
  Pallas kernels: 0 us -> 76.4 us
  starting transfers between devices: 78.7 us -> 10.9 us
  local copies, waits for them, and re-layouts: 33.4 us -> 75 us
  other arithmetic: 42.4 us -> 1.85 us
    ppermute x10 -> x9, waiting for transfers between devices: 509 us -> 221 us  [local(): received = lax.ppermute(sent, 'pipe', pairs)]
    dot_general x13 -> x1, matrix products: 154 us -> 14.7 us  [local(): lax.dot_general(mixed.reshape(-1, width), act.reshape(-1, width), (((0,),...]
    pallas_call x0 -> x11, Pallas kernels: none -> 76.4 us  [the longest x10 62.5 us: tick(): pl.pallas_call(tick_kernel, grid_spec=pltpu.PrefetchScalarGridSpec(num_sc...]
    unnamed x3 -> x104, local copies, waits for them, and re-layouts: 0.01 us -> 75 us
    ppermute x10 -> x9, starting transfers between devices: 78.7 us -> 10.9 us  [local(): received = lax.ppermute(sent, 'pipe', pairs)]
    convert_element_type x2 -> x0, other arithmetic: 20.7 us -> none  [the longest x1 20.7 us: local(): extra.astype(jnp.bfloat16)]
    broadcast_in_dim x2 -> x0, local copies, waits for them, and re-layouts: 14.2 us -> none  [the longest x1 12.5 us: local(): extra_init = jnp.zeros((width, width), jnp.float32)]
    reduce_scatter x1, waiting for transfers between devices: 159 us -> 170 us  [local(): lax.psum_scatter(partial.astype(jnp.bfloat16), 'dp', scatter_dimension=0,...]
  transfers between devices with their start and end apart: 11 -> 10, of which waited for: 11 -> 5; matrix products, arithmetic and copies ran while one was open for 0% -> 0% of each run, Pallas kernels for 0% -> 0%
where the time goes in v1:
time: 589 us; the launch traced here: 585 us
  waiting for transfers between devices  391 us (66%)
  Pallas kernels  76.4 us (13%)
  local copies, waits for them, and re-layouts  75 us (13%)
  matrix products  14.7 us (2%)
  between operations  14.5 us (2%)
  starting transfers between devices  10.9 us (2%)
    ppermute x9, waiting for transfers between devices, local(): received = lax.ppermute(sent, 'pipe', pairs)  221 us
    reduce_scatter x1, waiting for transfers between devices, local(): lax.psum_scatter(partial.astype(jnp.bfloat16), 'dp', scatter_dimension=0,...  170 us
    unnamed x104, local copies, waits for them, and re-layouts  75 us
    pallas_call x10, Pallas kernels, tick(): pl.pallas_call(tick_kernel, grid_spec=pltpu.PrefetchScalarGridSpec(num_sc...  62.5 us
    dot_general x1, matrix products, local(): lax.dot_general(mixed.reshape(-1, width), act.reshape(-1, width), (((0,),...  14.7 us
    pallas_call x1, Pallas kernels, recompute(): pl.pallas_call(recompute_kernel, grid=(width // block,), in_specs=[pl.Blo...  14 us
  transfers between devices with their start and end apart: 10, of which 5 were waited for; matrix products, arithmetic and copies ran while one was open for 0% of the time, Pallas kernels for 0%

profile of v1, /device:TPU:18, one launch (start us, length us, event | category | flops | bytes accessed | tf_op | source)
XLA Modules:
  0.0 584.6 jit_solution(13642368515659407036)
XLA Ops:
  11.5 14.0 %recompute.1 = (bf16[3,128,3072]{2,1,0:T(8,128)(2,1)S(1)}, f32[3,128,3072]{2,1,0:T(8,128)S(1)}, bf16[3,128,128]{2,1,0:T(8,128)(2,1)S(1)}, f32[3,128,128]{2,1,0:T...) custom-call(bf16[3,128,3072]{2,1,0:T(8,128)(2,1)S(1)} %bitcast.34, ...), custom_call_target="tpu_custom_call" | custom-call | flops 7247757312 | bytes 30670848 | tf_op jit(solution)/shard_map/recompute/pallas_call | solution.py:59
  25.5 4.4 tick.10
  33.0 2.3 copy-done.1
  38.7 2.5 tick.11
  44.3 2.3 copy-done.2
  50.0 2.5 tick.12
  55.6 2.3 copy-done.3
  61.3 2.5 tick.13
  67.1 2.3 copy-done.4
  72.8 2.5 tick.14
  78.4 2.3 copy-done.5
  84.1 2.5 tick.15
  90.3 177.3 %collective-permute-done.5.recv_ref = bf16[1,128,3072]{2,1,0:T(8,128)(2,1)S(1)} collective-permute-done((bf16[1,128,3072]{2,1,0:T(8,128)(2,1)}, bf16[1,128,3072]{2,1,0:T(8,128)(2,1)S(1)}, u32[]{:S(2)}, u32[]{:S(2)}) %collective-permute-start.5) | collective-permute-done | bytes 786464 | tf_op jit(solution)/shard_map/ppermute | solution.py:219
  267.6 2.3 copy-done.6
  273.3 13.5 %tick.16 = (bf16[1,128,3072]{2,1,0:T(8,128)(2,1)S(1)}, bf16[3,128,3072]{2,1,0:T(8,128)(2,1)}, bf16[3,128,3072]{2,1,0:T(8,128)(2,1)S(1)}) custom-call(s32[3]{0:T(128)S(1)} %add_add_fusion.3.sc_ref, bf16[1,128,3072]{2,1,0:T(8,128)(2,1)S(1)} %collective-permute-done.5.recv_ref, ...), custom_call_target="tpu_custom_call", output_to_operand_aliasing={{1}: (9, {}), {2}: (10, {})} | custom-call | flops 2415919104 | bytes 23592960 | tf_op jit(solution)/shard_map/tick/pallas_call | solution.py:150
  291.2 17.1 %collective-permute-done.6.recv_ref = bf16[1,128,3072]{2,1,0:T(8,128)(2,1)S(1)} collective-permute-done((bf16[1,128,3072]{2,1,0:T(8,128)(2,1)}, bf16[1,128,3072]{2,1,0:T(8,128)(2,1)S(1)}, u32[]{:S(2)}, u32[]{:S(2)}) %collective-permute-start.6) | collective-permute-done | bytes 786464 | tf_op jit(solution)/shard_map/ppermute | solution.py:219
  308.3 2.3 copy-done.7
  314.0 14.4 %tick.17 = (bf16[1,128,3072]{2,1,0:T(8,128)(2,1)}, bf16[3,128,3072]{2,1,0:T(8,128)(2,1)}, bf16[3,128,3072]{2,1,0:T(8,128)(2,1)S(1)}) custom-call(s32[3]{0:T(128)S(1)} %add_add_fusion.2.sc_ref, bf16[1,128,3072]{2,1,0:T(8,128)(2,1)S(1)} %collective-permute-done.6.recv_ref, ...), custom_call_target="tpu_custom_call", output_to_operand_aliasing={{1}: (9, {}), {2}: (10, {})} | custom-call | flops 2415919104 | bytes 23592960 | tf_op jit(solution)/shard_map/tick/pallas_call | solution.py:150
  331.9 15.0 %collective-permute-done.7.recv_ref = bf16[1,128,3072]{2,1,0:T(8,128)(2,1)S(1)} collective-permute-done((bf16[1,128,3072]{2,1,0:T(8,128)(2,1)}, bf16[1,128,3072]{2,1,0:T(8,128)(2,1)S(1)}, u32[]{:S(2)}, u32[]{:S(2)}) %collective-permute-start.7) | collective-permute-done | bytes 786464 | tf_op jit(solution)/shard_map/ppermute | solution.py:219
  352.5 14.4 %tick.18 = (bf16[1,128,3072]{2,1,0:T(8,128)(2,1)}, bf16[3,128,3072]{2,1,0:T(8,128)(2,1)}, bf16[3,128,3072]{2,1,0:T(8,128)(2,1)S(1)}) custom-call(s32[3]{0:T(128)S(1)} %add_add_fusion.1.sc_ref, bf16[1,128,3072]{2,1,0:T(8,128)(2,1)S(1)} %collective-permute-done.7.recv_ref, ...), custom_call_target="tpu_custom_call", output_to_operand_aliasing={{1}: (9, {}), {2}: (10, {})} | custom-call | flops 2415919104 | bytes 23592960 | tf_op jit(solution)/shard_map/tick/pallas_call | solution.py:150
  370.6 11.4 %collective-permute-done.8.recv_ref = bf16[1,128,3072]{2,1,0:T(8,128)(2,1)S(1)} collective-permute-done((bf16[1,128,3072]{2,1,0:T(8,128)(2,1)}, bf16[1,128,3072]{2,1,0:T(8,128)(2,1)S(1)}, u32[]{:S(2)}, u32[]{:S(2)}) %collective-permute-start.8) | collective-permute-done | bytes 786464 | tf_op jit(solution)/shard_map/ppermute | solution.py:219
  387.7 3.5 tick.19
  392.7 14.7 %bitcast_convert_fusion = bf16[3072,3072]{1,0:T(8,128)(2,1)} fusion(bf16[3,128,3072]{2,1,0:T(8,128)(2,1)S(1)} %copy-done.51, bf16[3,128,3072]{2,1,0:T(8,128)(2,1)} %copy-done.39), kind=kOutput, calls=%fused_computation | convolution fusion | flops 7257194496 | bytes 23592960 | tf_op jit(solution)/shard_map/dot_general | solution.py:221
  407.4 170.3 %reduce-scatter.2.cloned.1.call-done = bf16[192,3072]{1,0:T(8,128)(2,1)} async-done(((bf16[3072,3072]{1,0:T(8,128)(2,1)}), bf16[192,3072]{1,0:T(8,128)(2,1)}) %reduce-scatter.2.cloned.1.call-update) | async-done | bytes 1179664 | tf_op jit(solution)/shard_map/reduce_scatter | solution.py:223
  (126 shorter events, 71.5 us)
Async XLA Ops:
  7.2 570.6 %reduce-scatter.2.cloned.1.call-start = ((), (), s32[]{:S(2)}) async-start(), calls=%async_computation.1 | async-start | bytes 20054016 | tf_op jit(solution)/shard_map/reduce_scatter | solution.py:223
  11.5 14.0 %copy-start.10 = (bf16[3,128,3072]{2,1,0:T(8,128)(2,1)S(1)}, bf16[3,128,3072]{2,1,0:T(8,128)(2,1)}, u32[]{:S(2)}) copy-start(bf16[3,128,3072]{2,1,0:T(8,128)(2,1)} %up_ref.19) | copy-start | bytes 7077892
  25.4 4.4 copy-start
  25.5 4.4 copy-start.50
  25.5 7.6 %copy-start.41 = (f32[1,3072]{1,0:T(1,128)S(1)}, f32[1,3072]{1,0:T(1,128)}, u32[]{:S(2)}) copy-start(f32[1,3072]{1,0:T(1,128)} %gain_ref.21) | copy-start | bytes 36868
  32.2 0.8 collective-permute-start
  33.0 2.3 copy-start.1
  43.5 0.8 collective-permute-start.1
  44.3 2.3 copy-start.2
  54.8 0.8 collective-permute-start.2
  55.6 2.3 copy-start.3
  66.1 1.0 collective-permute-start.3
  67.1 2.3 copy-start.4
  77.6 0.8 collective-permute-start.4
  78.4 2.3 copy-start.5
  88.9 178.7 %collective-permute-start.5 = (bf16[1,128,3072]{2,1,0:T(8,128)(2,1)}, bf16[1,128,3072]{2,1,0:T(8,128)(2,1)S(1)}, u32[]{:S(2)}, u32[]{:S(2)}) collective-permute-start(bf16[1,128,3072]{2,1,0:T(8,128)(2,1)} %copy-done.44), channel_id=1, source_target_pairs={{32,16},{48,32},{64,48},{33,17},{49,33},{65,49},{34,18},{50,34},{6... | collective-permute-start | bytes 2359304 | tf_op jit(solution)/shard_map/ppermute | solution.py:219
  267.6 2.3 copy-start.6
  289.2 19.1 %collective-permute-start.6 = (bf16[1,128,3072]{2,1,0:T(8,128)(2,1)}, bf16[1,128,3072]{2,1,0:T(8,128)(2,1)S(1)}, u32[]{:S(2)}, u32[]{:S(2)}) collective-permute-start(bf16[1,128,3072]{2,1,0:T(8,128)(2,1)} %copy-done.48), channel_id=1, source_target_pairs={{16,0},{32,16},{48,32},{17,1},{33,17},{49,33},{18,2},{34,18},{50,3... | collective-permute-start | bytes 2359304 | tf_op jit(solution)/shard_map/ppermute | solution.py:219
  308.3 2.3 copy-start.7
  329.9 17.0 %collective-permute-start.7 = (bf16[1,128,3072]{2,1,0:T(8,128)(2,1)}, bf16[1,128,3072]{2,1,0:T(8,128)(2,1)S(1)}, u32[]{:S(2)}, u32[]{:S(2)}) collective-permute-start(bf16[1,128,3072]{2,1,0:T(8,128)(2,1)} %get-tuple-element.63), channel_id=1, source_target_pairs={{16,0},{32,16},{17,1},{33,17},{18,2},{34,18},{19,3},{35,19},{20,4}... | collective-permute-start | bytes 2359304 | tf_op jit(solution)/shard_map/ppermute | solution.py:219
  346.8 2.3 copy-start.8
  368.4 13.6 %collective-permute-start.8 = (bf16[1,128,3072]{2,1,0:T(8,128)(2,1)}, bf16[1,128,3072]{2,1,0:T(8,128)(2,1)S(1)}, u32[]{:S(2)}, u32[]{:S(2)}) collective-permute-start(bf16[1,128,3072]{2,1,0:T(8,128)(2,1)} %get-tuple-element.66), channel_id=1, source_target_pairs={{16,0},{17,1},{18,2},{19,3},{20,4},{21,5},{22,6},{23,7},{24,8},{25... | collective-permute-start | bytes 2359304 | tf_op jit(solution)/shard_map/ppermute | solution.py:219
  382.0 2.3 copy-start.9
  387.7 5.0 copy-start.51
  (38 other events, 54.0 us)
Sparse Core Ops, SparseCore 0:
  407.5 170.1 reduce-scatter.1
